TPU v7x, 128 devices: a whole 4x4x4 slice. The times are simulated.
128 devices in a mesh: subj: 4 (over x), fix: 32 (over z, y, core).
Axes of the slice: x: 4, y: 4, z: 4, core: 2. Of those that a mesh axis runs over, the one named last changes fastest.
Arguments:
- density: bfloat16 [1024, 65536], P(('subj', 'fix')), may hold values from -40 to 40, as said below
- conn_weight: bfloat16 [12288, 128, 128], P('fix'), may hold values from 9.983778e-07 to 1
- conn_rows: int32 [12288], P('fix'), may hold values from 0 to 16, as said below
- conn_cols: int32 [12288], P('fix'), may hold values from 0 to 47, as said below
- nbr_list: int32 [32, 32, 1], replicated, may hold values from 0 to 15
- design: int32 [1024, 64], P('subj'), may hold values from 0 to 15
Outputs:
- residual_scores: bfloat16 [1024, 65536], P('subj', 'fix')
- effect_scores: float32 [64, 65536], P(None, 'fix')
Inputs may be any that keep to these rules, and one draw needn't show every extreme that they name: density's subject rows follow global subject order; values lie within the range. Each owner's filled slots, over all senders, have pairwise different (conn_rows, conn_cols) pairs; some owner has every slot from every sender filled, and every owner has an empty one unless all of its slots are filled. `conn_cols`: codes below 16 name the owner's own blocks, higher codes 16 + h + k the neighbour block taken from holder h; empty slots carry a code too.
All inputs are finite; a program needn't handle non-finite values.
Results may differ from a plain program's by a relative error of at most 0.0049.
Values may be sent and summed in bfloat16 or wider, within the bound.
A program may use at most 128 MiB of HBM per device.

v0:
```python
import jax
import jax.numpy as jnp
from jax import lax
from jax.sharding import PartitionSpec as P

self_weight = 4.0
epsilon = 1e-06


def solve_normal(gram, right_side):
    factor = jnp.linalg.cholesky(gram)
    first = lax.linalg.triangular_solve(factor, right_side, left_side=True, lower=True)
    coefficients = lax.linalg.triangular_solve(
        factor, first, left_side=True, lower=True, transpose_a=True
    )
    identity = jnp.eye(gram.shape[0], dtype=gram.dtype)
    partial_inverse = lax.linalg.triangular_solve(factor, identity, left_side=True, lower=True)
    inverse = lax.linalg.triangular_solve(
        factor, partial_inverse, left_side=True, lower=True, transpose_a=True
    )
    return (coefficients, jnp.diagonal(inverse))


def shards(density, conn_weight, conn_rows, conn_cols, nbr_list, design):
    fix_count = lax.axis_size("fix")
    fix_index = lax.axis_index("fix")
    subj_count = lax.axis_size("subj")
    pre_rows, fixel_total = density.shape
    block_size = conn_weight.shape[-1]
    peer_blocks = nbr_list.shape[-1]
    blocks_dev = fixel_total // (fix_count * block_size)
    slot_cap = conn_weight.shape[0] // fix_count
    slot_total = fix_count * slot_cap
    source_count = blocks_dev + fix_count * peer_blocks
    subj_rows = pre_rows * fix_count
    weights, row_codes, col_codes = (
        lax.all_to_all(
            conn_weight.reshape(fix_count, slot_cap, block_size, block_size),
            "fix",
            split_axis=0,
            concat_axis=0,
            tiled=True,
        ),
        lax.all_to_all(
            conn_rows.reshape(fix_count, slot_cap), "fix", split_axis=0, concat_axis=0, tiled=True
        ),
        lax.all_to_all(
            conn_cols.reshape(fix_count, slot_cap), "fix", split_axis=0, concat_axis=0, tiled=True
        ),
    )
    weights = weights.reshape(slot_total, block_size, block_size)
    row_codes = row_codes.reshape(-1)
    col_codes = col_codes.reshape(-1)
    received = lax.all_to_all(
        density.reshape(pre_rows, fix_count, blocks_dev * block_size),
        "fix",
        split_axis=1,
        concat_axis=0,
        tiled=True,
    )
    own_blocks = received.reshape(subj_rows, blocks_dev, block_size)
    wanted = lax.dynamic_index_in_dim(nbr_list, fix_index, 1, keepdims=False).reshape(-1)
    outgoing = jnp.take(own_blocks, wanted, axis=1)
    arrived = lax.all_to_all(outgoing, "fix", split_axis=1, concat_axis=1, tiled=True)
    sources = jnp.concatenate([own_blocks, arrived], axis=1)
    filled = row_codes < blocks_dev
    col_index = jnp.where(filled, col_codes, source_count)
    row_index = jnp.where(filled, row_codes, 0)
    weight_table = jnp.zeros((source_count + 1, block_size, blocks_dev, block_size), weights.dtype)
    weight_table = weight_table.at[col_index, :, row_index, :].set(weights)
    weight_table = weight_table[:source_count].reshape(
        source_count * block_size, blocks_dev * block_size
    )
    spread = jnp.dot(
        sources.reshape(subj_rows, source_count * block_size),
        weight_table,
        preferred_element_type=jnp.float32,
    )
    own_wide = (
        sources[:, :blocks_dev, :].reshape(subj_rows, blocks_dev * block_size).astype(jnp.float32)
    )
    smoothed = (self_weight * own_wide + spread).astype(jnp.bfloat16)
    covariates = (design.astype(jnp.float32) - 7.5) * 0.25
    cov_half = covariates.astype(jnp.bfloat16)
    gram_part = jnp.dot(cov_half.T, cov_half, preferred_element_type=jnp.float32)
    cross_part = jnp.dot(cov_half.T, smoothed, preferred_element_type=jnp.float32)
    smoothed_wide = smoothed.astype(jnp.float32)
    gram_total, cross_total = lax.psum((gram_part, cross_part), "subj")
    coefficients, inverse_diag = solve_normal(gram_total, cross_total)
    residual = smoothed_wide - jnp.dot(covariates, coefficients, precision=lax.Precision.HIGHEST)
    squares = lax.psum(jnp.sum(residual * residual, axis=0), "subj")
    variance = squares / (subj_rows * subj_count - covariates.shape[1])
    scaling = lax.rsqrt(variance + epsilon)
    residual_scores = (residual * scaling[None, :]).astype(jnp.bfloat16)
    effect_scores = coefficients * scaling[None, :] * lax.rsqrt(inverse_diag)[:, None]
    return (residual_scores, effect_scores)


def solution(mesh):
    in_specs = (
        P(("subj", "fix"), None),
        P("fix", None, None),
        P("fix"),
        P("fix"),
        P(),
        P("subj", None),
    )
    out_specs = (P("subj", "fix"), P(None, "fix"))
    return jax.shard_map(shards, mesh=mesh, in_specs=in_specs, out_specs=out_specs, check_vma=False)
```

profile of v0, /device:TPU:0, one launch (start us, length us, event | category | flops | bytes accessed | tf_op | source)
XLA Modules:
  0.0 436.2 jit_solution(7345680927049764748)
XLA Ops:
  7.2 8.4 %all-to-all-start = ((bf16[8,32,2048]{2,0,1:T(8,128)(2,1)}), bf16[8,32,2048]{2,0,1:T(8,128)(2,1)S(1)}, u32[]{:S(2)}, u32[]{:S(2)}) async-start(bf16[8,32,2048]{2,0,1:T(8,128)(2,1)} %bitcast.60), calls=%async_computation | async-start | bytes 2097152 | tf_op jit(solution)/shard_map/all_to_all | solution.py:54
  15.6 1.4 all_to_all.33
  17.0 0.7 dynamic-slice_reduce_fusion
  17.8 15.2 %all-to-all-done = bf16[8,32,2048]{2,0,1:T(8,128)(2,1)S(1)} async-done(((bf16[8,32,2048]{2,0,1:T(8,128)(2,1)}), bf16[8,32,2048]{2,0,1:T(8,128)(2,1)S(1)}, u32[]{:S(2)}, u32[]{:S(2)}) %all-to-all-start) | async-done | bytes 1048608 | tf_op jit(solution)/shard_map/all_to_all | solution.py:54
  33.0 3.8 all-to-all-start.2
  36.8 1.4 all_to_all.35
  38.2 0.2 copy.28
  38.4 0.3 copy.20
  38.7 1.0 gather_fusion
  39.7 4.4 %all-to-all-done.2 = s32[32,1,12]{2,1,0:T(1,128)S(1)} async-done(((s32[32,1,12]{2,1,0:T(1,128)}), s32[32,1,12]{2,1,0:T(1,128)S(1)}, u32[]{:S(2)}, u32[]{:S(2)}) %all-to-all-start.2) | async-done | bytes 1568 | tf_op jit(solution)/shard_map/all_to_all | solution.py:44
  44.1 3.8 all-to-all-start.3
  47.9 1.6 select_bitcast_fusion
  49.5 5.7 %all-to-all-done.3 = s32[32,1,12]{2,1,0:T(1,128)S(1)} async-done(((s32[32,1,12]{2,1,0:T(1,128)}), s32[32,1,12]{2,1,0:T(1,128)S(1)}, u32[]{:S(2)}, u32[]{:S(2)}) %all-to-all-start.3) | async-done | bytes 1568 | tf_op jit(solution)/shard_map/all_to_all | solution.py:47
  55.2 32.6 %all_to_all.43 = bf16[256,32,128]{2,0,1:T(8,128)(2,1)S(1)} all-to-all(bf16[256,32,128]{2,0,1:T(8,128)(2,1)} %select_bitcast_fusion), channel_id=1, replica_groups=mesh['subj'=4,'fix'=32] {'fix'}, dimensions={1} | all-to-all | bytes 4194304 | tf_op jit(solution)/shard_map/all_to_all | solution.py:64
  87.8 5.2 %all-to-all-start.4 = ((bf16[32,12,128,128]{3,2,1,0:T(8,128)(2,1)}), bf16[32,12,128,128]{3,2,1,0:T(8,128)(2,1)}, u32[]{:S(2)}, u32[]{:S(2)}) async-start(bf16[32,12,128,128]{3,2,1,0:T(8,128)(2,1)} %bitcast.56), calls=%async_computation.4 | async-start | bytes 25165824 | tf_op jit(solution)/shard_map/all_to_all | solution.py:37
  93.0 0.0 all-reduce.2.cloned.1.call-start
  93.1 0.1 fusion.24
  93.2 17.1 %psum.21 = f32[64,64]{0,1:T(8,128)S(1)} all-reduce(f32[64,64]{0,1:T(8,128)S(1)} %fusion.24), channel_id=1, replica_groups=mesh['subj'=4,'fix'=32] {'subj'}, use_global_device_ids=true, to_apply=%region_1.2 | all-reduce | flops 4096 | bytes 32768 | tf_op jit(solution)/shard_map/psum | solution.py:88
  110.3 0.1 copy.26
  110.4 5.8 %cholesky.17 = f32[64,64]{1,0:T(8,128)S(1)} custom-call(f32[64,64]{1,0:T(8,128)S(1)} %fusion.19), custom_call_target="Cholesky" | custom-call | tf_op jit(solution)/shard_map/jit(cholesky)/cholesky | solution.py:11
  116.3 0.6 compare_reduce_fusion
  116.9 0.7 fusion.10
  117.6 4.9 %custom-call.12 = f32[1,64,64]{1,2,0:T(8,128)S(1)} custom-call(f32[1,64,64]{2,1,0:T(8,128)S(1)} %fusion.10), custom_call_target="InvertDiagBlocksLowerTriangular" | custom-call | tf_op jit(solution)/shard_map/triangular_solve | solution.py:13
  122.5 0.5 broadcast.243
  123.0 0.7 reduce.17
  123.7 0.1 reshape.159
  123.8 0.7 reduce.18
  124.5 0.1 reshape.160
  124.6 1.9 pad_maximum_fusion
  126.6 3.2 copy.21
  129.8 124.1 %all-to-all-done.4 = bf16[32,12,128,128]{3,2,1,0:T(8,128)(2,1)} async-done(((bf16[32,12,128,128]{3,2,1,0:T(8,128)(2,1)}), bf16[32,12,128,128]{3,2,1,0:T(8,128)(2,1)}, u32[]{:S(2)}, u32[]{:S(2)}) %all-to-all-start.4) | async-done | bytes 12582944 | tf_op jit(solution)/shard_map/all_to_all | solution.py:37
  253.8 8.9 %broadcast_in_dim.31 = bf16[49,128,16,128]{3,1,2,0:T(8,128)(2,1)} broadcast(bf16[]{:T(256)} %constant.94.clone.1), dimensions={} | broadcast | bytes 25690114 | tf_op jit(solution)/shard_map/broadcast_in_dim | solution.py:69
  262.7 64.0 %scatter_fusion = bf16[49,128,16,128]{3,1,2,0:T(8,128)(2,1)} fusion(bf16[49,128,16,128]{3,1,2,0:T(8,128)(2,1)} %broadcast_in_dim.31, s32[384]{0:T(512)S(1)} %fusion.27, bf16[384,128,128]{2,1,0:T(8,128)(2,1)} %bitcast.11), kind=kCustom, calls=%fused_computation.2 | custom fusion | bytes 37751808 | tf_op jit(solution)/shard_map/scatter | solution.py:70
  326.7 11.8 %slice.32 = bf16[48,128,16,128]{3,1,2,0:T(8,128)(2,1)S(1)} slice(bf16[49,128,16,128]{3,1,2,0:T(8,128)(2,1)} %scatter_fusion), slice={[0:48], [0:128], [0:16], [0:128]} | slice | bytes 50331648 | tf_op jit(solution)/shard_map/slice | solution.py:71
  338.5 17.6 %copy.24 = bf16[48,128,16,128]{3,2,1,0:T(8,128)(2,1)} copy(bf16[48,128,16,128]{3,1,2,0:T(8,128)(2,1)S(1)} %slice.32) | data formatting | bytes 50331648 | tf_op jit(solution)/shard_map/slice | solution.py:71
  356.1 11.9 %fusion.6 = bf16[256,2048]{1,0:T(8,128)(2,1)S(1)} fusion(bf16[256,6144]{0,1:T(8,128)(2,1)S(1)} %bitcast.59, bf16[768,8,16,128]{3,2,1,0:T(8,128)(2,1)} %bitcast.55, bf16[8,32,2048]{2,0,1:T(8,128)(2,1)S(1)} %copy-done.4), kind=kOutput, calls=%fused_computation.9 | convolution fusion | flops 6444548096 | bytes 30408704 | tf_op jit(solution)/shard_map/dot_general | solution.py:74
  368.0 1.0 copy-done.2
  368.9 1.1 fusion.22
  370.1 0.2 fusion.13
  370.3 0.2 fusion.11
  370.5 0.8 gather_fusion.1
  371.3 40.9 %all-reduce.2.cloned.1.call-done = f32[64,2048]{1,0:T(8,128)} async-done(((f32[64,2048]{1,0:T(8,128)}), f32[64,2048]{1,0:T(8,128)}) %all-reduce.2.cloned.1.call-update) | async-done | bytes 524304 | tf_op jit(solution)/shard_map/psum | solution.py:88
  412.2 1.7 fusion.17
  413.8 0.6 fusion.15
  414.4 3.3 multiply_reduce_fusion
  417.7 9.6 %psum.23 = f32[2048]{0:T(1024)S(1)} all-reduce(f32[2048]{0:T(1024)S(1)} %get-tuple-element.2), channel_id=1, replica_groups=mesh['subj'=4,'fix'=32] {'subj'}, use_global_device_ids=true, to_apply=%region_6.7 | all-reduce | flops 2048 | bytes 16384 | tf_op jit(solution)/shard_map/psum | solution.py:91
  427.3 0.9 multiply_multiply_fusion
  428.2 1.2 multiply_convert_fusion
  (21 shorter events, 0.2 us)
Async XLA Ops:
  7.2 9.9 %copy-start = (s32[32,32,1]{1,2,0:T(1,128)S(1)}, s32[32,32,1]{1,2,0:T(1,128)}, u32[]{:S(2)}) copy-start(s32[32,32,1]{1,2,0:T(1,128)} %param.10) | copy-start | bytes 12292
  7.2 25.8 %all-to-all-start = ((bf16[8,32,2048]{2,0,1:T(8,128)(2,1)}), bf16[8,32,2048]{2,0,1:T(8,128)(2,1)S(1)}, u32[]{:S(2)}, u32[]{:S(2)}) async-start(bf16[8,32,2048]{2,0,1:T(8,128)(2,1)} %bitcast.60), calls=%async_computation | async-start | bytes 2097152 | tf_op jit(solution)/shard_map/all_to_all | solution.py:54
  33.0 5.5 %copy-start.3 = (bf16[8,32,2048]{2,0,1:T(8,128)(2,1)}, bf16[8,32,2048]{2,0,1:T(8,128)(2,1)S(1)}, u32[]{:S(2)}) copy-start(bf16[8,32,2048]{2,0,1:T(8,128)(2,1)S(1)} %all-to-all-done) | copy-start | bytes 3145732
  33.0 11.1 %all-to-all-start.2 = ((s32[32,1,12]{2,1,0:T(1,128)}), s32[32,1,12]{2,1,0:T(1,128)S(1)}, u32[]{:S(2)}, u32[]{:S(2)}) async-start(s32[32,1,12]{2,1,0:T(1,128)} %bitcast.8), calls=%async_computation.2 | async-start | bytes 32768 | tf_op jit(solution)/shard_map/all_to_all | solution.py:44
  44.1 11.1 %all-to-all-start.3 = ((s32[32,1,12]{2,1,0:T(1,128)}), s32[32,1,12]{2,1,0:T(1,128)S(1)}, u32[]{:S(2)}, u32[]{:S(2)}) async-start(s32[32,1,12]{2,1,0:T(1,128)} %bitcast.9), calls=%async_computation.3 | async-start | bytes 32768 | tf_op jit(solution)/shard_map/all_to_all | solution.py:47
  87.8 5.3 %copy-start.5 = (s32[256,64]{0,1:T(8,128)S(1)}, s32[256,64]{0,1:T(8,128)}, u32[]{:S(2)}) copy-start(s32[256,64]{0,1:T(8,128)} %param.11) | copy-start | bytes 196612
  87.8 166.1 %all-to-all-start.4 = ((bf16[32,12,128,128]{3,2,1,0:T(8,128)(2,1)}), bf16[32,12,128,128]{3,2,1,0:T(8,128)(2,1)}, u32[]{:S(2)}, u32[]{:S(2)}) async-start(bf16[32,12,128,128]{3,2,1,0:T(8,128)(2,1)} %bitcast.56), calls=%async_computation.4 | async-start | bytes 25165824 | tf_op jit(solution)/shard_map/all_to_all | solution.py:37
  93.0 319.1 %all-reduce.2.cloned.1.call-start = ((), (), s32[]{:S(2)}) async-start(), calls=%async_computation.5 | async-start | bytes 1048576 | tf_op jit(solution)/shard_map/psum | solution.py:88
  338.5 17.6 %copy-start.4 = (bf16[8,32,2048]{2,0,1:T(8,128)(2,1)S(1)}, bf16[8,32,2048]{2,0,1:T(8,128)(2,1)}, u32[]{:S(2)}) copy-start(bf16[8,32,2048]{2,0,1:T(8,128)(2,1)} %copy-done.3) | copy-start | bytes 3145732
  368.0 1.0 copy-start.2
  413.8 15.5 %copy-start.1 = (s32[32,32,1]{1,2,0:T(1,128)S(1)}, s32[32,32,1]{1,2,0:T(1,128)}, u32[]{:S(2)}) copy-start(s32[32,32,1]{1,2,0:T(1,128)} %param.10) | copy-start | bytes 12292
Sparse Core Ops, SparseCore 0:
  370.2 41.9 all-reduce.1
where the time goes:
time: 438 us; the launch traced here: 436 us
  waiting for transfers between devices  190 us (43%)
  local copies, waits for them, and re-layouts  113 us (26%)
  blocking collectives  59.2 us (14%)
  starting transfers between devices  21.3 us (5%)
  other arithmetic  19.1 us (4%)
  matrix products  19 us (4%)
  between operations  14.3 us (3%)
    all_to_all x1, waiting for transfers between devices, shards(): lax.all_to_all(conn_weight.reshape(fix_count, slot_cap, block_size, block...  124 us
    scatter x1, local copies, waits for them, and re-layouts, shards(): weight_table = weight_table.at[col_index, :, row_index, :].set(weights)  64 us
    psum x1, waiting for transfers between devices, shards(): gram_total, cross_total = lax.psum((gram_part, cross_part), 'subj')  40.9 us
    all_to_all x1, blocking collectives, shards(): lax.all_to_all(outgoing, 'fix', split_axis=1, concat_axis=1, tiled=True)  32.6 us
    slice x2, local copies, waits for them, and re-layouts, shards(): weight_table[:source_count]  29.4 us
    psum x1, blocking collectives, shards(): gram_total, cross_total = lax.psum((gram_part, cross_part), 'subj')  17.1 us
    all_to_all x1, waiting for transfers between devices, shards(): lax.all_to_all(density.reshape(pre_rows, fix_count, blocks_dev * block_si...  15.2 us
    dot_general x1, matrix products, shards(): jnp.dot(sources.reshape(subj_rows, source_count * block_size), weight_tab...  11.9 us
  transfers between devices with their start and end apart: 5, of which 5 were waited for; matrix products, arithmetic and copies ran while one was open for 6% of the time, Pallas kernels for 0%

commit v1 on v0

v1 whole, which is shorter than its diff:
```python
import functools
import jax
import jax.numpy as jnp
from jax import lax
from jax.experimental import pallas as pl
from jax.experimental.pallas import tpu as pltpu
from jax.sharding import PartitionSpec as P

MESH = pl.DeviceIdType.MESH
SELF_WEIGHT = 4.0
EPSILON = 1e-06

NX, NF = 4, 32
BLOCK = 128
FB = 16
SRC = 48
CAP = 12
UNIT = 32
PER = BLOCK // UNIT
COV = 64
PEERS = NF - 1
PAIR = CAP * PER
QUART = 10
DIRECT = PAIR - 4 * QUART
NDIR = 2
LAG = 4
SLOTS = NF * CAP
COLS = FB * BLOCK
ROWS = 256
CHUNK = 2 * BLOCK
NCHUNK = COLS // CHUNK
GROUP = COLS // NX

_RING = ("01", "03", "10", "30", "11", "33", "13", "31", "20", "02", "12", "32", "21", "23", "22")
ORDER = [int(g[0]) * 8 + int(g[1]) * 2 + (c ^ (i & 1)) for c in (0, 1) for i, g in enumerate(_RING)] + [1]


def offset(k):
    words = [sum(v << (5 * i) for i, v in enumerate(ORDER[b : b + 6])) for b in range(0, PEERS, 6)]
    word = jnp.int32(words[0])
    for i in range(1, len(words)):
        word = jnp.where(k >= 6 * i, jnp.int32(words[i]), word)
    return (word >> (5 * lax.rem(k, 6))) & 31


def split(f):
    return f // 8, (f // 2) % 4, f % 2


def ahead(f, o):
    z, y, c = split(f)
    a, b, d = split(o)
    return lax.rem(z + a, 4) * 8 + lax.rem(y + b, 4) * 2 + lax.rem(c + d, 2)


def behind(f, o):
    z, y, c = split(f)
    a, b, d = split(o)
    return lax.rem(z + 4 - a, 4) * 8 + lax.rem(y + 4 - b, 4) * 2 + lax.rem(c + 2 - d, 2)


def remote(src, dst, send, recv, device):
    return pltpu.make_async_remote_copy(src, dst, send, recv, device_id=device, device_id_type=MESH)


def aligned(v, n):
    return pl.multiple_of(v, n)


def kernel(
    rows_ref, cols_ref, nbr_ref, dens_hbm, weight, design_t,
    scores, effects,
    dens, wbuf, stage, den, src, table, cstage, cbuf, idx_v, idx_s, gbuf, mat, linv, linvt, invd,
    smooth, resid, cov3, cpart, cin, bbuf, sqbuf,
    s_own, s_q, s_d, s_f, r_d, r_den, s_c, r_c, s_g, r_g, s_x, s_b, s_sq, r_sq,
    r_q, r_p, r_m, r_p2, r_m2, r_cin, r_b,
):
    x = lax.axis_index("subj")
    f = lax.axis_index("fix")
    xp, xm, x2 = lax.rem(x + 1, NX), lax.rem(x + 3, NX), lax.rem(x + 2, NX)
    half = QUART // 2
    dpart = DIRECT // NDIR

    own_dens = pltpu.make_async_copy(dens_hbm, dens, s_own.at[0])
    own_dens.start()
    own_rows = pl.ds(f * PAIR, PAIR)
    own_weight = pltpu.make_async_copy(weight.at[own_rows], wbuf.at[own_rows], s_own.at[1])
    own_weight.start()

    barrier = pltpu.get_barrier_semaphore()

    def greet(k, carry):
        pl.semaphore_signal(barrier, inc=1, device_id=(x, lax.rem(f + k, NF)), device_id_type=MESH)
        return carry

    lax.fori_loop(1, NF, greet, 0)
    for t in (xp, xm, x2):
        pl.semaphore_signal(barrier, inc=1, device_id=(t, f), device_id_type=MESH)
    pl.semaphore_wait(barrier, PEERS + 3)

    def send_quarter(i, carry):
        t = ahead(f, offset(i))
        remote(
            weight.at[pl.ds(t * PAIR + x * QUART, QUART)],
            wbuf.at[pl.ds(f * PAIR + x * QUART, QUART)],
            s_q, r_q.at[i], (x, t),
        ).start()
        return carry

    lax.fori_loop(0, PEERS, send_quarter, 0)

    cov_t = (design_t[...].astype(jnp.float32) - 7.5) * 0.25
    cov_wide = cov_t.T
    cov = cov_wide.astype(jnp.bfloat16)
    cov_half_t = cov_t.astype(jnp.bfloat16)
    for i in range(3):
        cov3[:, i * COV : (i + 1) * COV] = cov
    gbuf[x] = jnp.dot(cov_half_t, cov, preferred_element_type=jnp.float32)
    for t in (xp, xm, x2):
        remote(gbuf.at[x], gbuf.at[x], s_g, r_g, (t, f)).start()

    wbuf[SLOTS * PER :] = jnp.zeros((PER, UNIT, BLOCK), jnp.bfloat16)
    own_dens.wait()

    lane = lax.broadcasted_iota(jnp.int32, (8, BLOCK), 1)
    sub = lax.broadcasted_iota(jnp.int32, (8, BLOCK), 0)

    def gather_for(t):
        def own(c, carry):
            stage[t, c] = dens[t * FB + c]
            return carry

        def neighbour(h, carry):
            stage[t, FB + h] = dens[h * FB + nbr_ref[t, h]]
            return carry

        for c in range(FB):
            own(c, 0)
        for h in range(NF):
            neighbour(h, 0)
        codes = jnp.zeros((8, BLOCK), jnp.int32)
        for k in range(CAP):
            r = rows_ref[t * CAP + k]
            c = cols_ref[t * CAP + k]
            codes = jnp.where(lane == k, r * SRC + c, codes)
        cstage[t] = codes

    def send_side(i):
        t = ahead(f, offset(i))
        gather_for(t)
        remote(stage.at[t], den.at[f], s_d, r_den, (x, t)).start()
        remote(cstage.at[t], cbuf.at[f], s_c, r_c, (x, t)).start()

    def send_direct(i):
        t = ahead(f, offset(lax.rem(i, PEERS)))
        r = 4 * QUART + (i // PEERS) * dpart
        remote(
            weight.at[pl.ds(t * PAIR + r, dpart)],
            wbuf.at[pl.ds(f * PAIR + r, dpart)],
            s_d, r_d, (x, t),
        ).start()

    def pass_on(i):
        s = behind(f, offset(i))
        r = wbuf.at[pl.ds(s * PAIR + x * QUART, QUART)]
        remote(r, r, s_q, r_q.at[i], (x, f)).wait_recv()
        remote(r, r, s_f, r_p.at[i], (xp, f)).start()
        remote(r, r, s_f, r_m.at[i], (xm, f)).start()

    def pass_half(i):
        s = behind(f, offset(i))
        b = s * PAIR + xm * QUART
        r = wbuf.at[pl.ds(b, QUART)]
        remote(r, r, s_f, r_p.at[i], (xp, f)).wait_recv()
        r = wbuf.at[pl.ds(b, half)]
        remote(r, r, s_f, r_p2.at[i], (xp, f)).start()
        b = s * PAIR + xp * QUART
        r = wbuf.at[pl.ds(b, QUART)]
        remote(r, r, s_f, r_m.at[i], (xm, f)).wait_recv()
        r = wbuf.at[pl.ds(b + half, half)]
        remote(r, r, s_f, r_m2.at[i], (xm, f)).start()

    row_id = lax.broadcasted_iota(jnp.int32, (COV, 2 * COV), 0)
    lane_id = lax.broadcasted_iota(jnp.int32, (COV, 2 * COV), 1)

    def eliminate(j):
        m = mat[...]
        row = jnp.sum(jnp.where(row_id == j, m, 0.0), axis=0, keepdims=True)
        col = jnp.sum(jnp.where(lane_id == j, m, 0.0), axis=1, keepdims=True)
        pivot = jnp.sum(jnp.where((row_id == j) & (lane_id == j), m, 0.0), keepdims=True)
        factor = jnp.where(row_id > j, col / pivot, 0.0)
        mat[...] = m - factor * row

    def step(i, carry):
        @pl.when(i < PEERS)
        def _():
            pass_on(i)

        @pl.when(i >= LAG)
        def _():
            pass_half(i - LAG)

        @pl.when(i < PEERS)
        def _():
            send_side(i)
            for e in range(NDIR):
                send_direct(i * NDIR + e)

        return carry

    lax.fori_loop(0, PEERS + LAG, step, 0)

    whole = remote(gbuf.at[pl.ds(0, 3)], gbuf.at[pl.ds(0, 3)], s_g, r_g, (xp, f))
    whole.wait_recv()
    whole.wait_send()
    mat[:, :COV] = (gbuf[0] + gbuf[1]) + (gbuf[2] + gbuf[3])
    eye = (
        lax.broadcasted_iota(jnp.int32, (COV, COV), 0) == lax.broadcasted_iota(jnp.int32, (COV, COV), 1)
    )
    mat[:, COV:] = jnp.where(eye, 1.0, 0.0)

    def elim_step(j, carry):
        eliminate(j)
        return carry

    lax.fori_loop(0, COV, elim_step, 0)
    diag = jnp.sum(jnp.where(eye, mat[:, :COV], 0.0), axis=1, keepdims=True)
    lower = mat[:, COV:] / jnp.sqrt(diag)
    linv[...] = lower
    lower_t = lower.T
    linvt[...] = lower_t
    invd[...] = lax.rsqrt(jnp.sum(lower_t * lower_t, axis=1, keepdims=True))

    gather_for(f)
    den[f] = stage[f]
    cbuf[f] = cstage[f]
    rest = remote(cbuf.at[pl.ds(0, PEERS)], cbuf.at[pl.ds(0, PEERS)], s_c, r_c, (xp, f))
    rest.wait_recv()
    place = sub * BLOCK + lane

    def locate(s, acc):
        tile = cbuf[s]
        for k in range(CAP):
            acc = jnp.where(place == tile[:, k : k + 1], s * CAP + k, acc)
        return acc

    idx_v[...] = lax.fori_loop(0, NF, locate, jnp.full((8, BLOCK), SLOTS, jnp.int32))
    to_smem = pltpu.make_async_copy(idx_v, idx_s, s_own.at[0])
    to_smem.start()
    to_smem.wait()

    arrived = remote(den.at[pl.ds(0, PEERS)], den.at[pl.ds(0, PEERS)], s_d, r_den, (xp, f))
    arrived.wait_recv()

    def lay_out(c, carry):
        block = den[:, c].astype(jnp.float32).reshape(ROWS, BLOCK)
        src[:, pl.ds(aligned(c * BLOCK, BLOCK), BLOCK)] = block.astype(jnp.bfloat16)
        return carry

    lax.fori_loop(0, SRC, lay_out, 0)

    own_weight.wait()

    def last_halves(i, carry):
        r = wbuf.at[pl.ds(0, half)]
        remote(r, r, s_f, r_p2.at[i], (xp, f)).wait_recv()
        remote(r, r, s_f, r_m2.at[i], (xm, f)).wait_recv()
        return carry

    lax.fori_loop(0, PEERS, last_halves, 0)
    r = wbuf.at[pl.ds(0, PEERS * DIRECT)]
    remote(r, r, s_d, r_d, (xp, f)).wait_recv()

    def smooth_chunk(g):
        group = lax.rem(x + 1 + g // 2, NX)
        first = group * 4 + lax.rem(g, 2) * 2
        for c in range(SRC):
            for e in range(2):
                p = (first + e) * SRC + c
                i = idx_s[p // BLOCK, lax.rem(p, BLOCK)]
                for u in range(PER):
                    row = c * BLOCK + u * UNIT
                    table[row : row + UNIT, e * BLOCK : (e + 1) * BLOCK] = wbuf[i * PER + u]
        spread = jnp.dot(src[...], table[...], preferred_element_type=jnp.float32)
        at = pl.ds(aligned(first * BLOCK, BLOCK), CHUNK)
        part = (SELF_WEIGHT * src[:, at].astype(jnp.float32) + spread).astype(jnp.bfloat16)
        smooth[:, at] = part
        cpart[g] = jnp.dot(cov_half_t, part, preferred_element_type=jnp.float32)

    def send_chunk(g, carry):
        smooth_chunk(g)
        rel = g // 2
        remote(
            cpart.at[g], cin.at[rel, lax.rem(g, 2)], s_x, r_cin.at[g], (lax.rem(x + 1 + rel, NX), f)
        ).start()
        return carry

    lax.fori_loop(0, NCHUNK - 2, send_chunk, 0)

    def keep_chunk(g, carry):
        smooth_chunk(g)
        return carry

    lax.fori_loop(NCHUNK - 2, NCHUNK, keep_chunk, 0)

    for h in range(2):
        total = cpart[NCHUNK - 2 + h]
        for rel in range(3):
            remote(cpart.at[0], cin.at[rel, h], s_x, r_cin.at[rel * 2 + h], (xp, f)).wait_recv()
            total = total + cin[rel, h]
        y = jnp.dot(linv[...], total, preferred_element_type=jnp.float32, precision=lax.Precision.HIGHEST)
        bbuf[x, :, h * CHUNK : (h + 1) * CHUNK] = jnp.dot(
            linvt[...], y, preferred_element_type=jnp.float32, precision=lax.Precision.HIGHEST
        )
    for rel, t in enumerate((xp, x2, xm)):
        remote(bbuf.at[x], bbuf.at[x], s_b, r_b.at[rel], (t, f)).start()

    def residual(group):
        at = pl.ds(aligned(group * GROUP, GROUP), GROUP)
        beta = bbuf[group]
        b1 = beta.astype(jnp.bfloat16)
        left = beta - b1.astype(jnp.float32)
        b2 = left.astype(jnp.bfloat16)
        b3 = (left - b2.astype(jnp.float32)).astype(jnp.bfloat16)
        parts = jnp.concatenate([b1, b2, b3], axis=0)
        fitted = jnp.dot(cov3[...], parts, preferred_element_type=jnp.float32)
        res = smooth[:, at].astype(jnp.float32) - fitted
        resid[:, at] = res
        sqbuf[x, :, at] = jnp.sum(res * res, axis=0, keepdims=True)

    residual(x)
    for rel, t in enumerate((xm, x2, xp)):
        remote(bbuf.at[t], bbuf.at[t], s_b, r_b.at[rel], (t, f)).wait_recv()
        residual(t)
    for t in (xp, xm, x2):
        remote(sqbuf.at[x], sqbuf.at[x], s_sq, r_sq, (t, f)).start()
    whole = remote(sqbuf.at[pl.ds(0, 3)], sqbuf.at[pl.ds(0, 3)], s_sq, r_sq, (xp, f))
    whole.wait_recv()
    variance = ((sqbuf[0] + sqbuf[1]) + (sqbuf[2] + sqbuf[3])) / (ROWS * NX - COV)
    scaling = lax.rsqrt(variance + EPSILON)
    scores[...] = (resid[...] * scaling).astype(jnp.bfloat16)
    for g in range(NX):
        at = slice(g * GROUP, (g + 1) * GROUP)
        effects[:, at] = bbuf[g] * scaling[:, at] * invd[...]

    r = wbuf.at[pl.ds(0, PEERS * QUART)]
    remote(r, r, s_q, r_d, (xp, f)).wait_send()
    r = wbuf.at[pl.ds(0, 3 * PEERS * QUART)]
    remote(r, r, s_f, r_d, (xp, f)).wait_send()
    r = wbuf.at[pl.ds(0, PEERS * (DIRECT + SRC * 8 // UNIT))]
    remote(r, r, s_d, r_d, (xp, f)).wait_send()
    rest.wait_send()
    r = cpart.at[pl.ds(0, NCHUNK - 2)]
    remote(r, r, s_x, r_d, (xp, f)).wait_send()
    r = bbuf.at[pl.ds(0, 3)]
    remote(r, r, s_b, r_d, (xp, f)).wait_send()
    whole.wait_send()


def shards(density, conn_weight, conn_rows, conn_cols, nbr_list, design):
    dens = density.reshape(8, NF * FB, BLOCK).transpose(1, 0, 2)
    weight = conn_weight.reshape(NF * PAIR, UNIT, BLOCK)
    smem = pl.BlockSpec(memory_space=pltpu.SMEM)
    anywhere = pl.BlockSpec(memory_space=pl.ANY)
    vmem = pl.BlockSpec(memory_space=pltpu.VMEM)
    f32, bf16, i32 = jnp.float32, jnp.bfloat16, jnp.int32
    dma = pltpu.SemaphoreType.DMA
    return pl.pallas_call(
        kernel,
        out_shape=(
            jax.ShapeDtypeStruct((ROWS, COLS), bf16),
            jax.ShapeDtypeStruct((COV, COLS), f32),
        ),
        in_specs=[smem, smem, smem, anywhere, anywhere, vmem],
        out_specs=(vmem, vmem),
        scratch_shapes=[
            pltpu.VMEM((NF * FB, 8, BLOCK), bf16),
            pltpu.VMEM(((SLOTS + 1) * PER, UNIT, BLOCK), bf16),
            pltpu.VMEM((NF, SRC, 8, BLOCK), bf16),
            pltpu.VMEM((NF, SRC, 8, BLOCK), bf16),
            pltpu.VMEM((ROWS, SRC * BLOCK), bf16),
            pltpu.VMEM((SRC * BLOCK, CHUNK), bf16),
            pltpu.VMEM((NF, 8, BLOCK), i32),
            pltpu.VMEM((NF, 8, BLOCK), i32),
            pltpu.VMEM((8, BLOCK), i32),
            pltpu.SMEM((8, BLOCK), i32),
            pltpu.VMEM((NX, COV, COV), f32),
            pltpu.VMEM((COV, 2 * COV), f32),
            pltpu.VMEM((COV, COV), f32),
            pltpu.VMEM((COV, COV), f32),
            pltpu.VMEM((COV, 1), f32),
            pltpu.VMEM((ROWS, COLS), bf16),
            pltpu.VMEM((ROWS, COLS), f32),
            pltpu.VMEM((ROWS, 3 * COV), bf16),
            pltpu.VMEM((NCHUNK, COV, CHUNK), f32),
            pltpu.VMEM((3, 2, COV, CHUNK), f32),
            pltpu.VMEM((NX, COV, GROUP), f32),
            pltpu.VMEM((NX, 1, COLS), f32),
            dma((2,)),
        ]
        + [dma] * 13
        + [dma((PEERS,))] * 5
        + [dma((NCHUNK - 2,)), dma((3,))],
        compiler_params=pltpu.CompilerParams(
            collective_id=0, has_side_effects=True, vmem_limit_bytes=60 * 2**20
        ),
        cost_estimate=pl.CostEstimate(flops=2 * ROWS * SRC * BLOCK * COLS, bytes_accessed=30 << 20, transcendentals=0),
    )(conn_rows, conn_cols, nbr_list.reshape(NF, NF), dens, weight, design.T)


def solution(mesh):
    in_specs = (
        P(("subj", "fix"), None),
        P("fix", None, None),
        P("fix"),
        P("fix"),
        P(),
        P("subj", None),
    )
    out_specs = (P("subj", "fix"), P(None, "fix"))
    return jax.shard_map(shards, mesh=mesh, in_specs=in_specs, out_specs=out_specs, check_vma=False)
```

time: 438 us -> 141 us (0.32)
  waiting for transfers between devices: 190 us -> 0 us
  Pallas kernels: 0 us -> 136 us
  local copies, waits for them, and re-layouts: 113 us -> 4.18 us
  blocking collectives: 59.2 us -> 0 us
  starting transfers between devices: 21.3 us -> 0 us
  other arithmetic: 19.1 us -> 0 us
  matrix products: 19 us -> 0 us
  between operations: 14.3 us -> 0.64 us
    all_to_all x4 -> x0, waiting for transfers between devices: 149 us -> none  [the longest x1 124 us: shards(): lax.all_to_all(conn_weight.reshape(fix_count, slot_cap, block_size, block...]
    pallas_call x0 -> x1, Pallas kernels: none -> 136 us  [shards(): pl.pallas_call(kernel, out_shape=(jax.ShapeDtypeStruct((ROWS, COLS), bf16...]
    scatter x1 -> x0, local copies, waits for them, and re-layouts: 64 us -> none  [shards(): weight_table = weight_table.at[col_index, :, row_index, :].set(weights)]
    psum x1 -> x0, waiting for transfers between devices: 40.9 us -> none  [shards(): gram_total, cross_total = lax.psum((gram_part, cross_part), 'subj')]
    all_to_all x1 -> x0, blocking collectives: 32.6 us -> none  [shards(): lax.all_to_all(outgoing, 'fix', split_axis=1, concat_axis=1, tiled=True)]
    slice x2 -> x0, local copies, waits for them, and re-layouts: 29.4 us -> none  [shards(): weight_table[:source_count]]
    psum x2 -> x0, blocking collectives: 26.7 us -> none  [the longest x1 17.1 us: shards(): gram_total, cross_total = lax.psum((gram_part, cross_part), 'subj')]
    all_to_all x4 -> x0, starting transfers between devices: 21.3 us -> none  [the longest x1 8.43 us: shards(): lax.all_to_all(density.reshape(pre_rows, fix_count, blocks_dev * block_si...]
  transfers between devices with their start and end apart: 5 -> 0, of which waited for: 5 -> 0; matrix products, arithmetic and copies ran while one was open for 6% -> 0% of each run, Pallas kernels for 0% -> 0%
where the time goes in v1:
time: 141 us
  Pallas kernels  136 us (96%)
  local copies, waits for them, and re-layouts  4.18 us (3%)
    pallas_call x1, Pallas kernels, shards(): pl.pallas_call(kernel, out_shape=(jax.ShapeDtypeStruct((ROWS, COLS), bf16...  136 us
    unnamed x2, local copies, waits for them, and re-layouts  4.18 us

profile of v1, /device:TPU:0, one launch (start us, length us, event | category | flops | bytes accessed | tf_op | source)
XLA Modules:
  0.0 140.9 jit_solution(6129227246936543327)
XLA Ops:
  0.6 136.1 %shard_map.77 = (bf16[256,2048]{1,0:T(8,128)(2,1)}, f32[64,2048]{1,0:T(8,128)}) custom-call(s32[384]{0:T(512)} %rows_ref.1, s32[384]{0:T(512)} %cols_ref.1, s32[32,32]{1,0:T(8,128)} %bitcast.9, bf16[512,8,128]{2,1,0:T(8,128)(2,1)} %bitcast.7, bf16[1536,32,128]{2,1,0:T(8,128)(2,1)} %bitcast.6, s32[64,256]{1,0:T(8,128)} %bitcast.8), custom_call_target="tpu_custom_call" | custom-call | flops 6442450944 | bytes 31457280 | tf_op jit(solution)/shard_map/pallas_call | solution.py:368
  136.7 2.3 %copy.10 = bf16[256,2048]{1,0:T(8,128)(2,1)} copy(bf16[256,2048]{1,0:T(8,128)(2,1)} %get-tuple-element.4) | data formatting | bytes 2097152
  139.0 1.9 %copy.11 = f32[64,2048]{1,0:T(8,128)} copy(f32[64,2048]{1,0:T(8,128)} %get-tuple-element.5) | data formatting | bytes 1048576

commit v2 on v1

v2 whole, which is shorter than its diff:
```python
import functools
import jax
import jax.numpy as jnp
from jax import lax
from jax.experimental import pallas as pl
from jax.experimental.pallas import tpu as pltpu
from jax.sharding import PartitionSpec as P

MESH = pl.DeviceIdType.MESH
SELF_WEIGHT = 4.0
EPSILON = 1e-06

NX, NF = 4, 32
BLOCK = 128
FB = 16
SRC = 48
CAP = 12
UNIT = 32
PER = BLOCK // UNIT
COV = 64
PEERS = NF - 2
PAIR = CAP * PER
QUART = 10
DIRECT = PAIR - 4 * QUART
NDIR = 2
LAG = 4
ELIM_AT = 4
LAY_AT = 28
LAY_STEP = 8
KSTEP = 8
SLOTS = NF * CAP
COLS = FB * BLOCK
ROWS = 256
CHUNK = 2 * BLOCK
NCHUNK = COLS // CHUNK
GROUP = COLS // NX

_RING = ("01", "03", "10", "30", "11", "33", "13", "31", "20", "02", "12", "32", "21", "23", "22")
ORDER = [int(g[0]) * 8 + int(g[1]) * 2 + (c ^ (i & 1)) for c in (0, 1) for i, g in enumerate(_RING)]


def offset(k):
    words = [sum(v << (5 * i) for i, v in enumerate(ORDER[b : b + 6])) for b in range(0, PEERS, 6)]
    word = jnp.int32(words[0])
    for i in range(1, len(words)):
        word = jnp.where(k >= 6 * i, jnp.int32(words[i]), word)
    return (word >> (5 * lax.rem(k, 6))) & 31


def split(f):
    return f // 8, (f // 2) % 4, f % 2


def ahead(f, o):
    z, y, c = split(f)
    a, b, d = split(o)
    turn = 1 - 2 * c
    return lax.rem(z + 4 + turn * a, 4) * 8 + lax.rem(y + 4 + turn * b, 4) * 2 + lax.rem(c + d, 2)


def behind(f, o):
    z, y, c = split(f)
    a, b, d = split(o)
    sender = lax.rem(c + d, 2)
    turn = 1 - 2 * sender
    return lax.rem(z + 4 - turn * a, 4) * 8 + lax.rem(y + 4 - turn * b, 4) * 2 + sender


def remote(src, dst, send, recv, device):
    return pltpu.make_async_remote_copy(src, dst, send, recv, device_id=device, device_id_type=MESH)


def three(v):
    a = v.astype(jnp.bfloat16)
    v = v - a.astype(jnp.float32)
    b = v.astype(jnp.bfloat16)
    return a, b, (v - b.astype(jnp.float32)).astype(jnp.bfloat16)


def aligned(v, n):
    return pl.multiple_of(v, n)


def kernel(
    rows_ref, cols_ref, nbr_ref, dens_hbm, weight, design_t,
    resid_hbm, coef_hbm, scaling,
    dens, wbuf, stage, den, src, cstage, cbuf, idx_v, idx_s, gbuf, mat, solver, invd,
    smooth, resid, coef, cov3, cpart, cin, bbuf, sqbuf,
    s_own, s_q, s_d, s_f, r_d, r_den, s_g, r_g, s_x, s_b, s_sq, r_sq, s_out, s_sib, s_c, r_c,
    r_q, r_p, r_m, r_p2, r_m2, r_cin, r_b,
):
    x = lax.axis_index("subj")
    f = lax.axis_index("fix")
    xp, xm, x2 = lax.rem(x + 1, NX), lax.rem(x + 3, NX), lax.rem(x + 2, NX)
    half = QUART // 2
    dpart = DIRECT // NDIR

    own_dens = pltpu.make_async_copy(dens_hbm, dens, s_own.at[0])
    own_dens.start()
    own_rows = pl.ds(f * PAIR, PAIR)
    own_weight = pltpu.make_async_copy(weight.at[own_rows], wbuf.at[own_rows], s_own.at[1])
    own_weight.start()

    barrier = pltpu.get_barrier_semaphore()

    def greet(k, carry):
        pl.semaphore_signal(barrier, inc=1, device_id=(x, lax.rem(f + k, NF)), device_id_type=MESH)
        return carry

    lax.fori_loop(1, NF, greet, 0)
    for t in (xp, xm, x2):
        pl.semaphore_signal(barrier, inc=1, device_id=(t, f), device_id_type=MESH)
    pl.semaphore_wait(barrier, NF - 1 + 3)

    def send_quarter(i, carry):
        t = ahead(f, offset(i))
        remote(
            weight.at[pl.ds(t * PAIR + x * QUART, QUART)],
            wbuf.at[pl.ds(f * PAIR + x * QUART, QUART)],
            s_q, r_q.at[i], (x, t),
        ).start()
        return carry

    lax.fori_loop(0, PEERS, send_quarter, 0)

    sib = f + 1 - 2 * lax.rem(f, 2)

    def to_sibling():
        return remote(
            weight.at[pl.ds(sib * PAIR, PAIR)], wbuf.at[pl.ds(f * PAIR, PAIR)], s_sib.at[0], s_sib.at[1], (x, sib)
        )

    to_sibling().start()

    cov_t = (design_t[...].astype(jnp.float32) - 7.5) * 0.25
    cov_wide = cov_t.T
    cov = cov_wide.astype(jnp.bfloat16)
    cov_half_t = cov_t.astype(jnp.bfloat16)
    for i in range(3):
        cov3[:, i * COV : (i + 1) * COV] = cov
    gbuf[x] = jnp.dot(cov_half_t, cov, preferred_element_type=jnp.float32)
    for t in (xp, xm, x2):
        remote(gbuf.at[x], gbuf.at[x], s_g, r_g, (t, f)).start()

    wbuf[SLOTS * PER :] = jnp.zeros((PER, UNIT, BLOCK), jnp.bfloat16)
    own_dens.wait()

    lane = lax.broadcasted_iota(jnp.int32, (8, BLOCK), 1)
    sub = lax.broadcasted_iota(jnp.int32, (8, BLOCK), 0)

    def gather_for(t):
        def own(c, carry):
            stage[t, c] = dens[t * FB + c]
            return carry

        def neighbour(h, carry):
            stage[t, FB + h] = dens[h * FB + nbr_ref[t, h]]
            return carry

        for c in range(FB):
            own(c, 0)
        for h in range(NF):
            neighbour(h, 0)
    spot = sub * BLOCK + lane

    def codes_for(t):
        codes = jnp.zeros((1, BLOCK), jnp.int32)
        for k in range(CAP):
            code = rows_ref[t * CAP + k] * SRC + cols_ref[t * CAP + k]
            codes = jnp.where(lane[:1] == k, code, codes)
        return codes

    def send_side(t):
        gather_for(t)
        cstage[t] = codes_for(t)
        remote(cstage.at[t], cbuf.at[f], s_c, r_c, (x, t)).start()
        remote(stage.at[t], den.at[f], s_d, r_den, (x, t)).start()

    def send_direct(i):
        t = ahead(f, offset(lax.rem(i, PEERS)))
        r = 4 * QUART + (i // PEERS) * dpart
        remote(
            weight.at[pl.ds(t * PAIR + r, dpart)],
            wbuf.at[pl.ds(f * PAIR + r, dpart)],
            s_d, r_d, (x, t),
        ).start()

    def pass_on(i):
        s = behind(f, offset(i))
        r = wbuf.at[pl.ds(s * PAIR + x * QUART, QUART)]
        remote(r, r, s_q, r_q.at[i], (x, f)).wait_recv()
        remote(r, r, s_f, r_p.at[i], (xp, f)).start()
        remote(r, r, s_f, r_m.at[i], (xm, f)).start()

    def pass_half(i):
        s = behind(f, offset(i))
        b = s * PAIR + xm * QUART
        r = wbuf.at[pl.ds(b, QUART)]
        remote(r, r, s_f, r_p.at[i], (xp, f)).wait_recv()
        r = wbuf.at[pl.ds(b, half)]
        remote(r, r, s_f, r_p2.at[i], (xp, f)).start()
        b = s * PAIR + xp * QUART
        r = wbuf.at[pl.ds(b, QUART)]
        remote(r, r, s_f, r_m.at[i], (xm, f)).wait_recv()
        r = wbuf.at[pl.ds(b + half, half)]
        remote(r, r, s_f, r_m2.at[i], (xm, f)).start()

    row_id = lax.broadcasted_iota(jnp.int32, (COV, 2 * COV), 0)
    lane_id = lax.broadcasted_iota(jnp.int32, (COV, 2 * COV), 1)

    def eliminate(j):
        m = mat[...]
        row = jnp.sum(jnp.where(row_id == j, m, 0.0), axis=0, keepdims=True)
        col = jnp.sum(jnp.where(lane_id == j, m, 0.0), axis=1, keepdims=True)
        pivot = jnp.sum(jnp.where((row_id == j) & (lane_id == j), m, 0.0), keepdims=True)
        factor = jnp.where(row_id > j, col / pivot, 0.0)
        mat[...] = m - factor * row

    eye = (
        lax.broadcasted_iota(jnp.int32, (COV, COV), 0) == lax.broadcasted_iota(jnp.int32, (COV, COV), 1)
    )

    def all_gram():
        return remote(gbuf.at[pl.ds(0, 3)], gbuf.at[pl.ds(0, 3)], s_g, r_g, (xp, f))

    def all_codes():
        return remote(cbuf.at[pl.ds(0, NF - 1)], cbuf.at[pl.ds(0, NF - 1)], s_c, r_c, (xp, f))

    def locate(s, acc):
        tile = cbuf[s]
        for k in range(CAP):
            acc = jnp.where(spot == tile[:, k : k + 1], s * CAP + k, acc)
        return acc

    def lay_out(c):
        block = den[:, c].astype(jnp.float32).reshape(ROWS, BLOCK)
        src[:, pl.ds(aligned(c * BLOCK, BLOCK), BLOCK)] = block.astype(jnp.bfloat16)

    def step(i, carry):
        @pl.when(i < PEERS)
        def _():
            pass_on(i)

        @pl.when(i >= LAG)
        def _():
            pass_half(i - LAG)

        @pl.when(i < PEERS // 2)
        def _():
            for e in range(2):
                send_side(ahead(f, offset(2 * i + e)))

        @pl.when((i >= PEERS // 2) & (i < PEERS))
        def _():
            for e in range(2 * NDIR):
                send_direct((i - PEERS // 2) * 2 * NDIR + e)

        @pl.when(i == ELIM_AT - 1)
        def _():
            all_gram().wait_recv()
            mat[:, :COV] = (gbuf[0] + gbuf[1]) + (gbuf[2] + gbuf[3])
            mat[:, COV:] = jnp.where(eye, 1.0, 0.0)

        @pl.when((i >= ELIM_AT) & (i < ELIM_AT + COV // 4))
        def _():
            for e in range(4):
                eliminate((i - ELIM_AT) * 4 + e)

        @pl.when(i == ELIM_AT + COV // 4)
        def _():
            diag = jnp.sum(jnp.where(eye, mat[:, :COV], 0.0), axis=1, keepdims=True)
            lower = mat[:, COV:] / jnp.sqrt(diag)
            lower_t = lower.T
            inverse = jnp.dot(lower_t, lower, preferred_element_type=jnp.float32, precision=lax.Precision.HIGHEST)
            g1, g2, g3 = three(inverse)
            solver[...] = jnp.concatenate([g1, g1, g1, g2, g2, g3], axis=1)
            invd[...] = lax.rsqrt(jnp.sum(lower_t * lower_t, axis=1, keepdims=True))

        @pl.when(i == LAY_AT - 1)
        def _():
            all_codes().wait_recv()
            idx_v[...] = lax.fori_loop(0, NF, locate, jnp.full((8, BLOCK), SLOTS, jnp.int32))
            to_smem = pltpu.make_async_copy(idx_v, idx_s, s_own.at[0])
            to_smem.start()
            to_smem.wait()

        @pl.when(i == LAY_AT - 1)
        def _():
            remote(den.at[pl.ds(0, NF - 1)], den.at[pl.ds(0, NF - 1)], s_d, r_den, (xp, f)).wait_recv()

        for e in range(LAY_STEP):
            c = (i - LAY_AT) * LAY_STEP + e

            @pl.when((c >= 0) & (c < SRC))
            def _():
                lay_out(c)

        return carry

    send_side(sib)
    gather_for(f)
    den[f] = stage[f]
    cbuf[f] = codes_for(f)
    lax.fori_loop(0, PEERS + LAG, step, 0)

    own_weight.wait()
    to_sibling().wait_recv()

    def last_halves(i, carry):
        r = wbuf.at[pl.ds(0, half)]
        remote(r, r, s_f, r_p2.at[i], (xp, f)).wait_recv()
        remote(r, r, s_f, r_m2.at[i], (xm, f)).wait_recv()
        return carry

    lax.fori_loop(0, PEERS, last_halves, 0)
    r = wbuf.at[pl.ds(0, PEERS * DIRECT)]
    remote(r, r, s_d, r_d, (xp, f)).wait_recv()

    def smooth_pair(n, halves):
        firsts = [group * 4 + h * 2 for group, h in halves]

        def block(first, c):
            p = first * SRC + c
            i = idx_s[p // BLOCK, lax.rem(p, BLOCK)]
            return jnp.concatenate([wbuf[i * PER + u] for u in range(PER)], axis=0)

        spread = None
        for c0 in range(0, SRC, KSTEP):
            right = jnp.concatenate(
                [
                    jnp.concatenate([block(first + e, c) for first in firsts for e in range(2)], axis=1)
                    for c in range(c0, c0 + KSTEP)
                ],
                axis=0,
            )
            part = jnp.dot(
                src[:, c0 * BLOCK : (c0 + KSTEP) * BLOCK], right, preferred_element_type=jnp.float32
            )
            spread = part if spread is None else spread + part
        for e, first in enumerate(firsts):
            at = pl.ds(aligned(first * BLOCK, BLOCK), CHUNK)
            own = src[:, at].astype(jnp.float32)
            part = (SELF_WEIGHT * own + spread[:, e * CHUNK : (e + 1) * CHUNK]).astype(jnp.bfloat16)
            smooth[:, at] = part
            cpart[2 * n + e] = jnp.dot(cov_half_t, part, preferred_element_type=jnp.float32)

    def send_part(n, rel, h, t):
        remote(cpart.at[n], cin.at[rel, h], s_x, r_cin.at[rel * 2 + h], (t, f)).start()

    smooth_pair(0, ((x2, 0), (x2, 1)))
    send_part(0, 0, 0, x2)
    send_part(1, 0, 1, x2)
    for h in range(2):
        smooth_pair(1 + h, ((xp, h), (xm, h)))
        send_part(2 + 2 * h, 1, h, xp)
        send_part(3 + 2 * h, 2, h, xm)
    smooth_pair(3, ((x, 0), (x, 1)))

    for h in range(2):
        total = cpart[NCHUNK - 2 + h]
        for rel in range(3):
            remote(cpart.at[0], cin.at[rel, h], s_x, r_cin.at[rel * 2 + h], (xp, f)).wait_recv()
            total = total + cin[rel, h]
        t1, t2, t3 = three(total)
        right = jnp.concatenate([t1, t2, t3, t1, t2, t1], axis=0)
        bbuf[x, :, h * CHUNK : (h + 1) * CHUNK] = jnp.dot(solver[...], right, preferred_element_type=jnp.float32)
    for rel, t in enumerate((xp, xm, x2)):
        remote(bbuf.at[x], bbuf.at[x], s_b, r_b.at[rel], (t, f)).start()

    def residual(group):
        at = pl.ds(aligned(group * GROUP, GROUP), GROUP)
        beta = bbuf[group]
        parts = jnp.concatenate(three(beta), axis=0)
        fitted = jnp.dot(cov3[...], parts, preferred_element_type=jnp.float32)
        res = smooth[:, at].astype(jnp.float32) - fitted
        resid[group] = res
        pltpu.make_async_copy(resid.at[group], resid_hbm.at[:, at], s_out).start()
        sqbuf[x, :, at] = jnp.sum(res * res, axis=0, keepdims=True)

    residual(x)
    for rel, t in enumerate((xm, xp, x2)):
        remote(bbuf.at[t], bbuf.at[t], s_b, r_b.at[rel], (t, f)).wait_recv()
        residual(t)
    for t in (xp, xm, x2):
        remote(sqbuf.at[x], sqbuf.at[x], s_sq, r_sq, (t, f)).start()
    for g in range(NX):
        coef[:, g * GROUP : (g + 1) * GROUP] = bbuf[g] * invd[...]
    pltpu.make_async_copy(coef, coef_hbm, s_own.at[1]).start()
    whole = remote(sqbuf.at[pl.ds(0, 3)], sqbuf.at[pl.ds(0, 3)], s_sq, r_sq, (xp, f))
    whole.wait_recv()
    variance = ((sqbuf[0] + sqbuf[1]) + (sqbuf[2] + sqbuf[3])) / (ROWS * NX - COV)
    scaling[...] = lax.rsqrt(variance + EPSILON)

    pltpu.make_async_copy(resid, resid, s_out).wait()
    pltpu.make_async_copy(coef, coef_hbm, s_own.at[1]).wait()
    r = wbuf.at[pl.ds(0, PEERS * QUART)]
    remote(r, r, s_q, r_d, (xp, f)).wait_send()
    r = wbuf.at[pl.ds(0, 3 * PEERS * QUART)]
    remote(r, r, s_f, r_d, (xp, f)).wait_send()
    r = wbuf.at[pl.ds(0, PEERS * DIRECT + (NF - 1) * SRC * 8 // UNIT)]
    remote(r, r, s_d, r_d, (xp, f)).wait_send()
    to_sibling().wait_send()
    all_gram().wait_send()
    all_codes().wait_send()
    r = cpart.at[pl.ds(0, NCHUNK - 2)]
    remote(r, r, s_x, r_d, (xp, f)).wait_send()
    r = bbuf.at[pl.ds(0, 3)]
    remote(r, r, s_b, r_d, (xp, f)).wait_send()
    whole.wait_send()


def shards(density, conn_weight, conn_rows, conn_cols, nbr_list, design):
    dens = density.reshape(8, NF * FB, BLOCK).transpose(1, 0, 2)
    weight = conn_weight.reshape(NF * PAIR, UNIT, BLOCK)
    smem = pl.BlockSpec(memory_space=pltpu.SMEM)
    anywhere = pl.BlockSpec(memory_space=pl.ANY)
    vmem = pl.BlockSpec(memory_space=pltpu.VMEM)
    f32, bf16, i32 = jnp.float32, jnp.bfloat16, jnp.int32
    dma = pltpu.SemaphoreType.DMA
    residual, coefficients, scaling = pl.pallas_call(
        kernel,
        out_shape=(
            jax.ShapeDtypeStruct((ROWS, COLS), f32),
            jax.ShapeDtypeStruct((COV, COLS), f32),
            jax.ShapeDtypeStruct((1, COLS), f32),
        ),
        in_specs=[smem, smem, smem, anywhere, anywhere, vmem],
        out_specs=(anywhere, anywhere, vmem),
        scratch_shapes=[
            pltpu.VMEM((NF * FB, 8, BLOCK), bf16),
            pltpu.VMEM(((SLOTS + 1) * PER, UNIT, BLOCK), bf16),
            pltpu.VMEM((NF, SRC, 8, BLOCK), bf16),
            pltpu.VMEM((NF, SRC, 8, BLOCK), bf16),
            pltpu.VMEM((ROWS, SRC * BLOCK), bf16),
            pltpu.VMEM((NF, 1, BLOCK), i32),
            pltpu.VMEM((NF, 1, BLOCK), i32),
            pltpu.VMEM((8, BLOCK), i32),
            pltpu.SMEM((8, BLOCK), i32),
            pltpu.VMEM((NX, COV, COV), f32),
            pltpu.VMEM((COV, 2 * COV), f32),
            pltpu.VMEM((COV, 6 * COV), bf16),
            pltpu.VMEM((COV, 1), f32),
            pltpu.VMEM((ROWS, COLS), bf16),
            pltpu.VMEM((NX, ROWS, GROUP), f32),
            pltpu.VMEM((COV, COLS), f32),
            pltpu.VMEM((ROWS, 3 * COV), bf16),
            pltpu.VMEM((NCHUNK, COV, CHUNK), f32),
            pltpu.VMEM((3, 2, COV, CHUNK), f32),
            pltpu.VMEM((NX, COV, GROUP), f32),
            pltpu.VMEM((NX, 1, COLS), f32),
            dma((2,)),
        ]
        + [dma] * 12
        + [dma((2,)), dma, dma]
        + [dma((PEERS,))] * 5
        + [dma((NCHUNK - 2,)), dma((3,))],
        compiler_params=pltpu.CompilerParams(
            collective_id=0, has_side_effects=True, vmem_limit_bytes=60 * 2**20
        ),
        cost_estimate=pl.CostEstimate(flops=2 * ROWS * SRC * BLOCK * COLS, bytes_accessed=30 << 20, transcendentals=0),
    )(conn_rows, conn_cols, nbr_list.reshape(NF, NF), dens, weight, design.T)
    return (residual * scaling).astype(bf16), coefficients * scaling


def solution(mesh):
    in_specs = (
        P(("subj", "fix"), None),
        P("fix", None, None),
        P("fix"),
        P("fix"),
        P(),
        P("subj", None),
    )
    out_specs = (P("subj", "fix"), P(None, "fix"))
    return jax.shard_map(shards, mesh=mesh, in_specs=in_specs, out_specs=out_specs, check_vma=False)
```

time: 141 us -> 129 us (0.915)
  Pallas kernels: 136 us -> 124 us
  local copies, waits for them, and re-layouts: 4.18 us -> 0.01 us
  other arithmetic: 0 us -> 3.63 us
    pallas_call x1, Pallas kernels: 136 us -> 124 us  [shards(): pl.pallas_call(kernel, out_shape=(jax.ShapeDtypeStruct((ROWS, COLS), f32)...]
    unnamed x2 -> x4, local copies, waits for them, and re-layouts: 4.18 us -> 0.01 us
    convert_element_type x0 -> x1, other arithmetic: none -> 2.8 us  [shards(): return ((residual * scaling).astype(bf16), coefficients * scaling)]
where the time goes in v2:
time: 129 us; the launch traced here: 128 us
  Pallas kernels  124 us (96%)
  other arithmetic  3.63 us (3%)
    pallas_call x1, Pallas kernels, shards(): pl.pallas_call(kernel, out_shape=(jax.ShapeDtypeStruct((ROWS, COLS), f32)...  124 us
    convert_element_type x1, other arithmetic, shards(): return ((residual * scaling).astype(bf16), coefficients * scaling)  2.8 us

profile of v2, /device:TPU:0, one launch (start us, length us, event | category | flops | bytes accessed | tf_op | source)
XLA Modules:
  0.0 128.4 jit_solution(17036108094760480603)
XLA Ops:
  0.6 124.1 %shard_map.77 = (f32[256,2048]{1,0:T(8,128)}, f32[64,2048]{1,0:T(8,128)}, f32[1,2048]{1,0:T(1,128)}) custom-call(s32[384]{0:T(512)} %rows_ref.1, s32[384]{0:T(512)} %cols_ref.1, s32[32,32]{1,0:T(8,128)} %bitcast.12, bf16[512,8,128]{2,1,0:T(8,128)(2,1)} %bitcast.10, bf16[1536,32,128]{2,1,0:T(8,128)(2,1)} %bitcast.9, s32[64,256]{1,0:T(8,128)} %bitcast.11), custom_call_target="tpu_custom_call" | custom-call | flops 6442450944 | bytes 31457280 | tf_op jit(solution)/shard_map/pallas_call | solution.py:420
  124.7 0.0 copy-start
  124.7 0.0 copy-start.1
  124.7 2.8 %multiply_convert_fusion = bf16[256,2048]{1,0:T(8,128)(2,1)} fusion(f32[256,2048]{1,0:T(8,128)} %get-tuple-element.5, f32[2048]{0:T(1024)} %bitcast.7), kind=kLoop, calls=%fused_computation | loop fusion | flops 1048576 | bytes 3153920 | tf_op jit(solution)/shard_map/convert_element_type | solution.py:462
  127.5 0.0 copy-done
  127.5 0.0 copy-done.1
  127.5 0.8 broadcast_multiply_fusion
Async XLA Ops:
  124.7 2.8 %copy-start = (f32[64,2048]{1,0:T(8,128)S(1)}, f32[64,2048]{1,0:T(8,128)}, u32[]{:S(2)}) copy-start(f32[64,2048]{1,0:T(8,128)} %get-tuple-element.7) | copy-start | bytes 1572868
  124.7 2.8 %copy-start.1 = (f32[1,2048]{1,0:T(1,128)S(1)}, f32[1,2048]{1,0:T(1,128)}, u32[]{:S(2)}) copy-start(f32[1,2048]{1,0:T(1,128)} %get-tuple-element.6) | copy-start | bytes 24580

commit v3 on v2

--- a/solution.py
+++ b/solution.py
@@ -83,10 +83,10 @@
 
 def kernel(
     rows_ref, cols_ref, nbr_ref, dens_hbm, weight, design_t,
-    resid_hbm, coef_hbm, scaling,
+    resid, coef, scaling,
     dens, wbuf, stage, den, src, cstage, cbuf, idx_v, idx_s, gbuf, mat, solver, invd,
-    smooth, resid, coef, cov3, cpart, cin, bbuf, sqbuf,
-    s_own, s_q, s_d, s_f, r_d, r_den, s_g, r_g, s_x, s_b, s_sq, r_sq, s_out, s_sib, s_c, r_c,
+    smooth, cov3, cpart, cin, bbuf, sqbuf,
+    s_own, s_q, s_d, s_f, r_d, r_den, s_g, r_g, s_x, s_b, s_sq, r_sq, s_sib, s_c, r_c,
     r_q, r_p, r_m, r_p2, r_m2, r_cin, r_b,
 ):
     x = lax.axis_index("subj")
@@ -373,8 +373,7 @@
         parts = jnp.concatenate(three(beta), axis=0)
         fitted = jnp.dot(cov3[...], parts, preferred_element_type=jnp.float32)
         res = smooth[:, at].astype(jnp.float32) - fitted
-        resid[group] = res
-        pltpu.make_async_copy(resid.at[group], resid_hbm.at[:, at], s_out).start()
+        resid[:, at] = res
         sqbuf[x, :, at] = jnp.sum(res * res, axis=0, keepdims=True)
 
     residual(x)
@@ -385,14 +384,11 @@
         remote(sqbuf.at[x], sqbuf.at[x], s_sq, r_sq, (t, f)).start()
     for g in range(NX):
         coef[:, g * GROUP : (g + 1) * GROUP] = bbuf[g] * invd[...]
-    pltpu.make_async_copy(coef, coef_hbm, s_own.at[1]).start()
     whole = remote(sqbuf.at[pl.ds(0, 3)], sqbuf.at[pl.ds(0, 3)], s_sq, r_sq, (xp, f))
     whole.wait_recv()
     variance = ((sqbuf[0] + sqbuf[1]) + (sqbuf[2] + sqbuf[3])) / (ROWS * NX - COV)
     scaling[...] = lax.rsqrt(variance + EPSILON)
 
-    pltpu.make_async_copy(resid, resid, s_out).wait()
-    pltpu.make_async_copy(coef, coef_hbm, s_own.at[1]).wait()
     r = wbuf.at[pl.ds(0, PEERS * QUART)]
     remote(r, r, s_q, r_d, (xp, f)).wait_send()
     r = wbuf.at[pl.ds(0, 3 * PEERS * QUART)]
@@ -409,6 +405,21 @@
     whole.wait_send()
 
 
+def scale(residual, coefficients, scaling, scores, effects, half_scores, half_effects, sems):
+    by = scaling[...]
+    part = ROWS // NX
+    copies = [pltpu.make_async_copy(half_effects, effects, sems.at[NX])]
+    half_effects[...] = coefficients[...] * by
+    copies[0].start()
+    for i in range(NX):
+        rows = pl.ds(i * part, part)
+        half_scores[i] = (residual[rows, :] * by).astype(jnp.bfloat16)
+        copies.append(pltpu.make_async_copy(half_scores.at[i], scores.at[rows], sems.at[i]))
+        copies[-1].start()
+    for copy in copies:
+        copy.wait()
+
+
 def shards(density, conn_weight, conn_rows, conn_cols, nbr_list, design):
     dens = density.reshape(8, NF * FB, BLOCK).transpose(1, 0, 2)
     weight = conn_weight.reshape(NF * PAIR, UNIT, BLOCK)
@@ -420,12 +431,12 @@
     residual, coefficients, scaling = pl.pallas_call(
         kernel,
         out_shape=(
-            jax.ShapeDtypeStruct((ROWS, COLS), f32),
-            jax.ShapeDtypeStruct((COV, COLS), f32),
-            jax.ShapeDtypeStruct((1, COLS), f32),
+            pltpu.VMEM((ROWS, COLS), f32),
+            pltpu.VMEM((COV, COLS), f32),
+            pltpu.VMEM((1, COLS), f32),
         ),
         in_specs=[smem, smem, smem, anywhere, anywhere, vmem],
-        out_specs=(anywhere, anywhere, vmem),
+        out_specs=(vmem, vmem, vmem),
         scratch_shapes=[
             pltpu.VMEM((NF * FB, 8, BLOCK), bf16),
             pltpu.VMEM(((SLOTS + 1) * PER, UNIT, BLOCK), bf16),
@@ -441,8 +452,6 @@
             pltpu.VMEM((COV, 6 * COV), bf16),
             pltpu.VMEM((COV, 1), f32),
             pltpu.VMEM((ROWS, COLS), bf16),
-            pltpu.VMEM((NX, ROWS, GROUP), f32),
-            pltpu.VMEM((COV, COLS), f32),
             pltpu.VMEM((ROWS, 3 * COV), bf16),
             pltpu.VMEM((NCHUNK, COV, CHUNK), f32),
             pltpu.VMEM((3, 2, COV, CHUNK), f32),
@@ -450,16 +459,24 @@
             pltpu.VMEM((NX, 1, COLS), f32),
             dma((2,)),
         ]
-        + [dma] * 12
+        + [dma] * 11
         + [dma((2,)), dma, dma]
         + [dma((PEERS,))] * 5
         + [dma((NCHUNK - 2,)), dma((3,))],
         compiler_params=pltpu.CompilerParams(
-            collective_id=0, has_side_effects=True, vmem_limit_bytes=60 * 2**20
+            collective_id=0, has_side_effects=True, vmem_limit_bytes=56 * 2**20
         ),
         cost_estimate=pl.CostEstimate(flops=2 * ROWS * SRC * BLOCK * COLS, bytes_accessed=30 << 20, transcendentals=0),
     )(conn_rows, conn_cols, nbr_list.reshape(NF, NF), dens, weight, design.T)
-    return (residual * scaling).astype(bf16), coefficients * scaling
+
+    return pl.pallas_call(
+        scale,
+        out_shape=(jax.ShapeDtypeStruct((ROWS, COLS), bf16), jax.ShapeDtypeStruct((COV, COLS), f32)),
+        in_specs=[vmem, vmem, vmem],
+        out_specs=(anywhere, anywhere),
+        scratch_shapes=[pltpu.VMEM((NX, ROWS // NX, COLS), bf16), pltpu.VMEM((COV, COLS), f32), dma((NX + 1,))],
+        compiler_params=pltpu.CompilerParams(vmem_limit_bytes=16 * 2**20),
+    )(residual, coefficients, scaling)
 
 
 def solution(mesh):

time: 129 us -> 126 us (0.977)
  other arithmetic: 3.63 us -> 0 us
    convert_element_type x1 -> x0, other arithmetic: 2.8 us -> none  [shards(): return ((residual * scaling).astype(bf16), coefficients * scaling)]
    pallas_call x1 -> x2, Pallas kernels: 124 us -> 125 us  [the longest x1 123 us: shards(): pl.pallas_call(kernel, out_shape=(pltpu.VMEM((ROWS, COLS), f32), pltpu.VM...]
where the time goes in v3:
time: 126 us; the launch traced here: 125 us
  Pallas kernels  125 us (99%)
    pallas_call x1, Pallas kernels, shards(): pl.pallas_call(kernel, out_shape=(pltpu.VMEM((ROWS, COLS), f32), pltpu.VM...  123 us

profile of v3, /device:TPU:0, one launch (start us, length us, event | category | flops | bytes accessed | tf_op | source)
XLA Modules:
  0.0 125.3 jit_solution(18364135556679342883)
XLA Ops:
  0.6 123.5 %shard_map.77 = (f32[256,2048]{1,0:T(8,128)S(1)}, f32[64,2048]{1,0:T(8,128)S(1)}, f32[1,2048]{1,0:T(1,128)S(1)}) custom-call(s32[384]{0:T(512)} %rows_ref.1, s32[384]{0:T(512)} %cols_ref.1, s32[32,32]{1,0:T(8,128)} %bitcast.9, bf16[512,8,128]{2,1,0:T(8,128)(2,1)} %bitcast.7, bf16[1536,32,128]{2,1,0:T(8,128)(2,1)} %bitcast.6, s32[64,256]{1,0:T(8,128)} %bitcast.8), custom_call_target="tpu_custom_call" | custom-call | flops 6442450944 | bytes 31457280 | tf_op jit(solution)/shard_map/pallas_call | solution.py:431
  124.1 1.2 shard_map.78

commit v4 on v3

--- a/solution.py
+++ b/solution.py
@@ -342,53 +342,59 @@
             own = src[:, at].astype(jnp.float32)
             part = (SELF_WEIGHT * own + spread[:, e * CHUNK : (e + 1) * CHUNK]).astype(jnp.bfloat16)
             smooth[:, at] = part
-            cpart[2 * n + e] = jnp.dot(cov_half_t, part, preferred_element_type=jnp.float32)
+            cpart[n + e] = jnp.dot(cov_half_t, part, preferred_element_type=jnp.float32)
 
     def send_part(n, rel, h, t):
         remote(cpart.at[n], cin.at[rel, h], s_x, r_cin.at[rel * 2 + h], (t, f)).start()
 
-    smooth_pair(0, ((x2, 0), (x2, 1)))
-    send_part(0, 0, 0, x2)
-    send_part(1, 0, 1, x2)
-    for h in range(2):
-        smooth_pair(1 + h, ((xp, h), (xm, h)))
-        send_part(2 + 2 * h, 1, h, xp)
-        send_part(3 + 2 * h, 2, h, xm)
-    smooth_pair(3, ((x, 0), (x, 1)))
-
-    for h in range(2):
-        total = cpart[NCHUNK - 2 + h]
+    def half_beta(slot, h, rel, t):
+        return remote(bbuf.at[slot, h], bbuf.at[slot, h], s_b, r_b.at[2 * rel + h], (t, f))
+
+    def solve(h):
+        total = cpart[4 * h + 3]
         for rel in range(3):
             remote(cpart.at[0], cin.at[rel, h], s_x, r_cin.at[rel * 2 + h], (xp, f)).wait_recv()
             total = total + cin[rel, h]
         t1, t2, t3 = three(total)
         right = jnp.concatenate([t1, t2, t3, t1, t2, t1], axis=0)
-        bbuf[x, :, h * CHUNK : (h + 1) * CHUNK] = jnp.dot(solver[...], right, preferred_element_type=jnp.float32)
-    for rel, t in enumerate((xp, xm, x2)):
-        remote(bbuf.at[x], bbuf.at[x], s_b, r_b.at[rel], (t, f)).start()
-
-    def residual(group):
-        at = pl.ds(aligned(group * GROUP, GROUP), GROUP)
-        beta = bbuf[group]
-        parts = jnp.concatenate(three(beta), axis=0)
+        bbuf[x, h] = jnp.dot(solver[...], right, preferred_element_type=jnp.float32)
+        half_beta(x, h, 2, x2).start()
+        half_beta(x, h, 0, xp).start()
+        half_beta(x, h, 1, xm).start()
+
+    smooth_pair(0, ((x2, 0), (xp, 0)))
+    send_part(0, 0, 0, x2)
+    send_part(1, 1, 0, xp)
+    smooth_pair(2, ((xm, 0), (x, 0)))
+    send_part(2, 2, 0, xm)
+    smooth_pair(4, ((x2, 1), (xp, 1)))
+    send_part(4, 0, 1, x2)
+    send_part(5, 1, 1, xp)
+    smooth_pair(6, ((xm, 1),))
+    send_part(6, 2, 1, xm)
+    solve(0)
+    smooth_pair(7, ((x, 1),))
+    solve(1)
+
+    def residual(group, h):
+        at = pl.ds(aligned(group * GROUP + h * CHUNK, CHUNK), CHUNK)
+        parts = jnp.concatenate(three(bbuf[group, h]), axis=0)
         fitted = jnp.dot(cov3[...], parts, preferred_element_type=jnp.float32)
         res = smooth[:, at].astype(jnp.float32) - fitted
         resid[:, at] = res
         sqbuf[x, :, at] = jnp.sum(res * res, axis=0, keepdims=True)
 
-    residual(x)
-    for rel, t in enumerate((xm, xp, x2)):
-        remote(bbuf.at[t], bbuf.at[t], s_b, r_b.at[rel], (t, f)).wait_recv()
-        residual(t)
+    for h in range(2):
+        residual(x, h)
+        for rel, t in enumerate((xm, xp, x2)):
+            half_beta(t, h, rel, t).wait_recv()
+            residual(t, h)
     for t in (xp, xm, x2):
         remote(sqbuf.at[x], sqbuf.at[x], s_sq, r_sq, (t, f)).start()
     for g in range(NX):
-        coef[:, g * GROUP : (g + 1) * GROUP] = bbuf[g] * invd[...]
+        for h in range(2):
+            coef[:, g * GROUP + h * CHUNK : g * GROUP + (h + 1) * CHUNK] = bbuf[g, h] * invd[...]
     whole = remote(sqbuf.at[pl.ds(0, 3)], sqbuf.at[pl.ds(0, 3)], s_sq, r_sq, (xp, f))
-    whole.wait_recv()
-    variance = ((sqbuf[0] + sqbuf[1]) + (sqbuf[2] + sqbuf[3])) / (ROWS * NX - COV)
-    scaling[...] = lax.rsqrt(variance + EPSILON)
-
     r = wbuf.at[pl.ds(0, PEERS * QUART)]
     remote(r, r, s_q, r_d, (xp, f)).wait_send()
     r = wbuf.at[pl.ds(0, 3 * PEERS * QUART)]
@@ -402,6 +408,10 @@
     remote(r, r, s_x, r_d, (xp, f)).wait_send()
     r = bbuf.at[pl.ds(0, 3)]
     remote(r, r, s_b, r_d, (xp, f)).wait_send()
+    whole.wait_recv()
+    variance = ((sqbuf[0] + sqbuf[1]) + (sqbuf[2] + sqbuf[3])) / (ROWS * NX - COV)
+    scaling[...] = lax.rsqrt(variance + EPSILON)
+
     whole.wait_send()
 
 
@@ -455,14 +465,14 @@
             pltpu.VMEM((ROWS, 3 * COV), bf16),
             pltpu.VMEM((NCHUNK, COV, CHUNK), f32),
             pltpu.VMEM((3, 2, COV, CHUNK), f32),
-            pltpu.VMEM((NX, COV, GROUP), f32),
+            pltpu.VMEM((NX, 2, COV, CHUNK), f32),
             pltpu.VMEM((NX, 1, COLS), f32),
             dma((2,)),
         ]
         + [dma] * 11
         + [dma((2,)), dma, dma]
         + [dma((PEERS,))] * 5
-        + [dma((NCHUNK - 2,)), dma((3,))],
+        + [dma((NCHUNK - 2,)), dma((6,))],
         compiler_params=pltpu.CompilerParams(
             collective_id=0, has_side_effects=True, vmem_limit_bytes=56 * 2**20
         ),

time: 126 us -> 125 us (level)
  Pallas kernels: 125 us -> 123 us
    pallas_call x1, Pallas kernels: 123 us -> 122 us  [shards(): pl.pallas_call(kernel, out_shape=(pltpu.VMEM((ROWS, COLS), f32), pltpu.VM...]
where the time goes in v4:
time: 125 us; the launch traced here: 124 us
  Pallas kernels  123 us (98%)
    pallas_call x1, Pallas kernels, shards(): pl.pallas_call(kernel, out_shape=(pltpu.VMEM((ROWS, COLS), f32), pltpu.VM...  122 us

profile of v4, /device:TPU:0, one launch (start us, length us, event | category | flops | bytes accessed | tf_op | source)
XLA Modules:
  0.0 123.6 jit_solution(5659574073655083443)
XLA Ops:
  0.6 121.8 %shard_map.77 = (f32[256,2048]{1,0:T(8,128)S(1)}, f32[64,2048]{1,0:T(8,128)S(1)}, f32[1,2048]{1,0:T(1,128)S(1)}) custom-call(s32[384]{0:T(512)} %rows_ref.1, s32[384]{0:T(512)} %cols_ref.1, s32[32,32]{1,0:T(8,128)} %bitcast.9, bf16[512,8,128]{2,1,0:T(8,128)(2,1)} %bitcast.7, bf16[1536,32,128]{2,1,0:T(8,128)(2,1)} %bitcast.6, s32[64,256]{1,0:T(8,128)} %bitcast.8), custom_call_target="tpu_custom_call" | custom-call | flops 6442450944 | bytes 31457280 | tf_op jit(solution)/shard_map/pallas_call | solution.py:441
  122.4 1.2 shard_map.78
